TPU v7x, 32 devices: a whole 2x2x4 slice. The times are simulated.
32 devices in a mesh: rows: 8 (over z, x), seq: 4 (over y, core).
Axes of the slice: x: 2, y: 2, z: 4, core: 2. Of those that a mesh axis runs over, the one named last changes fastest.
Arguments:
- frames_in: bfloat16 [16, 4096, 512], P('rows', 'seq'), may hold values from -6 to 6
- lengths: int32 [16, 4], P('rows'), may hold values from 1 to 2048, 4096 in all within a row
- bw_ids: int32 [16, 4], P('rows'), may hold values from 0 to 3
- owner_list: int32 [137], replicated, may hold values from 0 to 7, as said below
- master: float32 [216, 32, 512], P('rows')
- moment1: float32 [216, 32, 512], P('rows')
- moment2: float32 [216, 32, 512], P('rows'), as said below
- wave_grad: bfloat16 [16, 1310720], P('rows', 'seq'), may hold values from -6 to 6
Outputs:
- waveform: float32 [16, 1310720], P('rows', 'seq')
- input_grad: float32 [16, 4096, 512], P('rows', 'seq')
- new_master: float32 [216, 32, 512], P('rows')
- new_moment1: float32 [216, 32, 512], P('rows')
- new_moment2: float32 [216, 32, 512], P('rows')
Inputs may be any that keep to these rules, and one draw needn't show every extreme that they name: `owner_list`: no index along rows owns more than 27 buckets, and some index owns exactly 27. `moment2`: every entry is positive.
All inputs are finite; a program needn't handle non-finite values.
Results may differ from a plain program's by a relative error of at most 0.012.
The roundings to bfloat16 on the way count: a program that leaves them out, or rounds other values in their place, can miss the bound.
Values may be sent and summed in bfloat16 or wider, within the bound.
No kernel may reach another device: no remote copies, remote signals or barrier semaphores. Data moves between devices by JAX's collectives and lax.ppermute only.
A program may use at most 192 MiB of HBM per device.

v0:
```python
import math
import jax
import jax.numpy as jnp
from jax import lax
from jax.sharding import PartitionSpec as P

FF = 1536
NFFT = 1280
HOP = 320
NBW = 4
KW = 7
UTT = 4
BR = 32
STEP_COUNT = 6
BINS = 641
NOUT = 1282
VROWS = 20
IN_ROWS = 3
HEAD_ROWS = 3
PR = 4380
NB = 137
NORM_EPS = 1e-06
ENV_FLOOR = 0.5
BETA_ONE = 0.8
BETA_TWO = 0.9
LEARN_RATE = 0.04
WEIGHT_DECAY = 0.01
ADAM_EPS = 1e-08


def padded(block, sides, width):
    for axis, dim in sides:
        count = lax.axis_size(axis)
        forward = [(i, i + 1) for i in range(count - 1)]
        backward = [(target, source) for source, target in forward]
        low = lax.ppermute(
            lax.slice_in_dim(block, block.shape[dim] - width, None, axis=dim), axis, forward
        )
        high = lax.ppermute(lax.slice_in_dim(block, 0, width, axis=dim), axis, backward)
        block = jnp.concatenate([low, block, high], axis=dim)
    return block


def from_behind(block, axis, distance):
    devices = range(lax.axis_size(axis))
    route = [(i - distance, i) for i in devices if i - distance in devices]
    return lax.ppermute(block, axis, route)


def slot_maps(owner_list, owner_count, slot_count):
    bucket_count = owner_list.shape[0]
    bucket_index = jnp.arange(bucket_count, dtype=jnp.int32)
    same_owner = owner_list[None, :] == owner_list[:, None]
    before = bucket_index[None, :] < bucket_index[:, None]
    slot_rank = jnp.sum((same_owner & before).astype(jnp.int32), axis=1)
    bucket_place = owner_list * slot_count + slot_rank
    targets = jnp.arange(owner_count * slot_count, dtype=jnp.int32)
    slot_match = bucket_place[None, :] == targets[:, None]
    found_bucket = jnp.sum(slot_match.astype(jnp.int32) * bucket_index[None, :], axis=1)
    source = jnp.where(jnp.any(slot_match, axis=1), found_bucket, bucket_count)
    return (bucket_place, source)


def synthesis_table():
    bin_index = jnp.arange(BINS, dtype=jnp.int32)[:, None]
    tap_index = jnp.arange(NFFT, dtype=jnp.int32)[None, :]
    turns = bin_index * tap_index % NFFT
    angle = turns.astype(jnp.float32) * (2.0 * math.pi / NFFT)
    edge_bin = (bin_index == 0) | (bin_index == NFFT // 2)
    factor = jnp.where(edge_bin, 1.0, 2.0).astype(jnp.float32) / NFFT
    return jnp.concatenate([factor * jnp.cos(angle), -factor * jnp.sin(angle)], axis=0)


def hann_window():
    angle = jnp.arange(NFFT, dtype=jnp.int32).astype(jnp.float32) * (2.0 * math.pi / NFFT)
    return 0.5 - 0.5 * jnp.cos(angle)


def segment_ids(lengths, first_index, span):
    starts = jnp.cumsum(lengths, axis=1) - lengths
    frame_index = first_index + jnp.arange(span, dtype=jnp.int32)
    return jnp.sum((starts[:, None, :] <= frame_index[None, :, None]).astype(jnp.int32), axis=2) - 1


def layer_norm(values):
    row_mean = jnp.mean(values, axis=-1, keepdims=True)
    centered = values - row_mean
    return centered * lax.rsqrt(jnp.mean(centered * centered, axis=-1, keepdims=True) + NORM_EPS)


def ada_norm(values, scale_rows, shift_rows):
    return layer_norm(values) * scale_rows + shift_rows


def final_norm(values, norm_gain, norm_bias):
    return layer_norm(values) * norm_gain[None, :] + norm_bias[None, :]


def exact_gelu(values):
    return jax.nn.gelu(values, approximate=False)


def contract(left_side, right_side, left_dim, right_dim):
    return lax.dot_general(
        left_side,
        right_side,
        (((left_dim,), (right_dim,)), ((), ())),
        preferred_element_type=jnp.float32,
    )


def local(frames_in, lengths, bw_ids, owner_list, master, moment1, moment2, wave_grad):
    rows_here, frames_here, channels = frames_in.shape
    slot_count = master.shape[0]
    frame_count = rows_here * frames_here
    lap_count = NFFT // HOP
    rim_width = (KW - 1) // 2
    margin = max(rim_width, lap_count - 1)
    bucket_place, source = slot_maps(owner_list, lax.axis_size("rows"), slot_count)
    gathered = lax.all_gather(master.astype(jnp.bfloat16), "rows", axis=0, tiled=True)
    buckets = jnp.take(gathered, bucket_place, axis=0)
    weight_table = buckets.reshape(-1, channels)[:PR]
    w_in = weight_table[:FF]
    w_out = weight_table[FF : 2 * FF]
    w_head = weight_table[2 * FF : 2 * FF + NOUT]
    row_start = 2 * FF + NOUT
    channel_rows = weight_table[row_start : row_start + VROWS].astype(jnp.float32)
    row_start = row_start + VROWS
    bias_in = weight_table[row_start : row_start + IN_ROWS].reshape(-1).astype(jnp.float32)
    row_start = row_start + IN_ROWS
    bias_head = (
        weight_table[row_start : row_start + HEAD_ROWS].reshape(-1)[:NOUT].astype(jnp.float32)
    )
    conv_weight = channel_rows[:KW]
    conv_bias = channel_rows[KW]
    ada_scale = channel_rows[KW + 1 : KW + 1 + NBW]
    ada_shift = channel_rows[KW + 1 + NBW : KW + 1 + 2 * NBW]
    vec_base = KW + 1 + 2 * NBW
    bias_out = channel_rows[vec_base]
    layer_scale = channel_rows[vec_base + 1]
    norm_gain = channel_rows[vec_base + 2]
    norm_bias = channel_rows[vec_base + 3]
    first_index = lax.axis_index("seq") * frames_here - margin
    segment = segment_ids(lengths, first_index, frames_here + 2 * margin)
    own_segment = segment[:, margin : margin + frames_here]
    halo_frames = padded(frames_in, (("seq", 1),), rim_width)
    wide_frames = halo_frames.astype(jnp.float32)
    conv_keep = []
    conv_out = jnp.zeros((rows_here, frames_here, channels), jnp.float32) + conv_bias
    for tap_index in range(KW):
        lower = margin - rim_width + tap_index
        keep = (segment[:, lower : lower + frames_here] == own_segment).astype(jnp.float32)[
            :, :, None
        ]
        conv_keep.append(keep)
        conv_out = (
            conv_out
            + keep * wide_frames[:, tap_index : tap_index + frames_here] * conv_weight[tap_index]
        )
    conv_out = conv_out.reshape(frame_count, channels)
    utt_pick = (own_segment[:, :, None] == jnp.arange(UTT, dtype=jnp.int32)[None, None, :]).astype(
        jnp.int32
    )
    frame_ids = jnp.sum(utt_pick * bw_ids[:, None, :], axis=2).reshape(frame_count)
    bw_onehot = (frame_ids[:, None] == jnp.arange(NBW, dtype=jnp.int32)[None, :]).astype(
        jnp.float32
    )
    scale_rows = jnp.dot(bw_onehot, ada_scale, precision=lax.Precision.HIGHEST)
    shift_rows = jnp.dot(bw_onehot, ada_shift, precision=lax.Precision.HIGHEST)
    ada_value, ada_back = jax.vjp(ada_norm, conv_out, scale_rows, shift_rows)
    ada_low = ada_value.astype(jnp.bfloat16)
    hidden_pre = contract(ada_low, w_in, 1, 1) + bias_in[None, :]
    act_value, gelu_back = jax.vjp(exact_gelu, hidden_pre)
    act_low = act_value.astype(jnp.bfloat16)
    branch = contract(act_low, w_out, 1, 0) + bias_out[None, :]
    frames_flat = frames_in.reshape(frame_count, channels).astype(jnp.float32)
    residual = frames_flat + layer_scale[None, :] * branch
    normed_value, final_back = jax.vjp(final_norm, residual, norm_gain, norm_bias)
    normed_low = normed_value.astype(jnp.bfloat16)
    head_out = contract(normed_low, w_head, 1, 1) + bias_head[None, :]
    magnitude = jnp.exp(head_out[:, :BINS])
    phase_angle = head_out[:, BINS:]
    real_part = magnitude * jnp.cos(phase_angle)
    imag_part = magnitude * jnp.sin(phase_angle)
    spectrum_low = jnp.concatenate([real_part, imag_part], axis=1).astype(jnp.bfloat16)
    synthesis = synthesis_table().astype(jnp.bfloat16)
    signal = contract(spectrum_low, synthesis, 1, 0)
    window_rows = hann_window().reshape(lap_count, HOP)
    pieces = signal.reshape(rows_here, frames_here, lap_count, HOP) * window_rows[None, None, :, :]
    lap_keep = []
    numerator = jnp.zeros((rows_here, frames_here + lap_count - 1, HOP), jnp.float32)
    envelope = jnp.zeros((rows_here, frames_here, HOP), jnp.float32)
    for lap_index in range(lap_count):
        ahead = margin + lap_index
        keep = (segment[:, ahead : ahead + frames_here] == own_segment).astype(jnp.float32)[
            :, :, None
        ]
        lap_keep.append(keep)
        numerator = numerator + jnp.pad(
            keep * pieces[:, :, lap_index], ((0, 0), (lap_index, lap_count - 1 - lap_index), (0, 0))
        )
        behind = margin - lap_index
        back_keep = (segment[:, behind : behind + frames_here] == own_segment).astype(jnp.float32)[
            :, :, None
        ]
        envelope = envelope + back_keep * (window_rows[lap_index] ** 2)[None, None, :]
    arrived = from_behind(numerator[:, frames_here:], "seq", 1)
    numerator = numerator[:, :frames_here] + jnp.pad(
        arrived, ((0, 0), (0, frames_here - lap_count + 1), (0, 0))
    )
    denominator = jnp.maximum(envelope, ENV_FLOOR)
    waveform = (numerator / denominator).reshape(rows_here, frames_here * HOP)
    scaled = wave_grad.astype(jnp.float32).reshape(rows_here, frames_here, HOP) / denominator
    later_rows = from_behind(scaled[:, : lap_count - 1], "seq", -1)
    reach_rows = jnp.concatenate([scaled, later_rows], axis=1)
    signal_grad = jnp.stack(
        [
            lap_keep[lap_index]
            * window_rows[lap_index][None, None, :]
            * reach_rows[:, lap_index : lap_index + frames_here]
            for lap_index in range(lap_count)
        ],
        axis=2,
    )
    signal_low = signal_grad.reshape(frame_count, NFFT).astype(jnp.bfloat16)
    spec_grad = contract(signal_low, synthesis, 1, 1)
    real_grad = spec_grad[:, :BINS]
    imag_grad = spec_grad[:, BINS:]
    head_grad = jnp.concatenate(
        [
            real_grad * real_part + imag_grad * imag_part,
            imag_grad * real_part - real_grad * imag_part,
        ],
        axis=1,
    ).astype(jnp.bfloat16)
    grad_w_head = contract(head_grad, normed_low, 0, 0)
    grad_b_head = jnp.sum(head_grad, axis=0, dtype=jnp.float32)
    normed_grad = contract(head_grad, w_head, 1, 0)
    residual_grad, grad_gain, grad_bias = final_back(normed_grad)
    branch_low = (layer_scale[None, :] * residual_grad).astype(jnp.bfloat16)
    grad_layer_scale = jnp.sum(residual_grad * branch, axis=0)
    grad_w_out = contract(act_low, branch_low, 0, 0)
    grad_b_out = jnp.sum(branch_low, axis=0, dtype=jnp.float32)
    act_grad = contract(branch_low, w_out, 1, 1)
    pre_low = gelu_back(act_grad)[0].astype(jnp.bfloat16)
    grad_w_in = contract(pre_low, ada_low, 0, 0)
    grad_b_in = jnp.sum(pre_low, axis=0, dtype=jnp.float32)
    ada_grad = contract(pre_low, w_in, 1, 0)
    conv_grad, scale_grad_rows, shift_grad_rows = ada_back(ada_grad)
    grad_scales = lax.dot_general(
        bw_onehot, scale_grad_rows, (((0,), (0,)), ((), ())), precision=lax.Precision.HIGHEST
    )
    grad_shifts = lax.dot_general(
        bw_onehot, shift_grad_rows, (((0,), (0,)), ((), ())), precision=lax.Precision.HIGHEST
    )
    conv_rows = conv_grad.reshape(rows_here, frames_here, channels)
    grad_conv_b = jnp.sum(conv_grad, axis=0)
    grad_conv_w = jnp.stack(
        [
            jnp.sum(
                conv_keep[tap_index]
                * conv_rows
                * wide_frames[:, tap_index : tap_index + frames_here],
                axis=(0, 1),
            )
            for tap_index in range(KW)
        ],
        axis=0,
    )
    halo_grad = padded(conv_rows, (("seq", 1),), rim_width)
    input_grad = residual_grad.reshape(rows_here, frames_here, channels)
    for tap_index in range(KW):
        lower = margin + rim_width - tap_index
        keep = (segment[:, lower : lower + frames_here] == own_segment).astype(jnp.float32)[
            :, :, None
        ]
        begin = 2 * rim_width - tap_index
        input_grad = (
            input_grad + conv_weight[tap_index] * keep * halo_grad[:, begin : begin + frames_here]
        )
    vec_grads = jnp.concatenate(
        [
            grad_conv_w,
            grad_conv_b[None, :],
            grad_scales,
            grad_shifts,
            jnp.stack([grad_b_out, grad_layer_scale, grad_gain, grad_bias], axis=0),
        ],
        axis=0,
    )
    in_rows = grad_b_in.reshape(IN_ROWS, channels)
    head_rows = jnp.pad(grad_b_head, (0, HEAD_ROWS * channels - NOUT)).reshape(HEAD_ROWS, channels)
    grad_table = jnp.concatenate(
        [grad_w_in, grad_w_out, grad_w_head, vec_grads, in_rows, head_rows], axis=0
    )
    grad_buckets = jnp.pad(grad_table, ((0, NB * BR - PR), (0, 0))).reshape(NB, BR, channels)
    empty_bucket = jnp.zeros((1, BR, channels), jnp.float32)
    summed = lax.psum(grad_buckets, ("rows", "seq"))
    extended = jnp.concatenate([summed, empty_bucket], axis=0)
    my_sources = lax.dynamic_slice_in_dim(source, lax.axis_index("rows") * slot_count, slot_count)
    reduced = jnp.take(extended, my_sources, axis=0)
    first_new = BETA_ONE * moment1 + (1.0 - BETA_ONE) * reduced
    second_new = BETA_TWO * moment2 + (1.0 - BETA_TWO) * reduced * reduced
    first_fix = 1.0 - BETA_ONE**STEP_COUNT
    second_fix = 1.0 - BETA_TWO**STEP_COUNT
    master_new = master - LEARN_RATE * (
        first_new / first_fix / (jnp.sqrt(second_new / second_fix) + ADAM_EPS)
        + WEIGHT_DECAY * master
    )
    return (waveform, input_grad, master_new, first_new, second_new)


def solution(mesh):
    in_specs = (
        P("rows", "seq", None),
        P("rows", None),
        P("rows", None),
        P(),
        P("rows", None, None),
        P("rows", None, None),
        P("rows", None, None),
        P("rows", "seq"),
    )
    out_specs = (
        P("rows", "seq"),
        P("rows", "seq", None),
        P("rows", None, None),
        P("rows", None, None),
        P("rows", None, None),
    )
    return jax.shard_map(local, mesh=mesh, in_specs=in_specs, out_specs=out_specs, check_vma=False)
```

profile of v0, /device:TPU:0, one launch (start us, length us, event | category | flops | bytes accessed | tf_op | source)
XLA Modules:
  0.0 546.3 jit_solution(15566940357598605938)
XLA Ops:
  35.9 15.2 %multiply_convert_fusion.2 = (bf16[641,1280]{1,0:T(8,128)(2,1)}, bf16[641,1280]{1,0:T(8,128)(2,1)}) fusion(f32[641]{0:T(1024)S(1)} %fusion.74, f32[641]{0:T(1024)S(1)} %select_multiply_fusion), kind=kLoop, calls=%fused_computation.89 | loop fusion | flops 10666240 | bytes 3287048 | tf_op jit(solution)/shard_map/convert.12
  51.9 9.4 %concatenate.35 = bf16[2,1030,512]{2,1,0:T(8,128)(2,1)S(1)} concatenate(bf16[2,3,512]{2,1,0:T(4,128)(2,1)S(1)} %collective-permute-done, bf16[2,1024,512]{2,1,0:T(8,128)(2,1)} %param.8, bf16[2,3,512]{2,1,0:T(4,128)(2,1)S(1)} %collective-permute-done.1), dimensions={1} | concatenate | bytes 4218880 | tf_op jit(solution)/shard_map/concatenate | solution.py:40
  71.7 10.2 %copy.40 = bf16[2,1024,4,320]{1,0,3,2:T(2,128)(2,1)} copy(bf16[2,1024,4,320]{1,3,0,2:T(8,128)(2,1)} %pad_maximum_fusion.1) | data formatting | bytes 10485760 | tf_op jit(solution)/shard_map/stack | solution.py:216
  86.7 9.7 %fusion.49 = f32[2048,1282]{0,1:T(8,128)} fusion(bf16[2048,1280]{0,1:T(8,128)(2,1)S(1)} %bitcast.122, bf16[641,1280]{1,0:T(8,128)(2,1)S(1)} %copy-done.20, bf16[641,1280]{1,0:T(8,128)(2,1)S(1)} %copy-done.21), kind=kOutput, calls=%fused_computation.122 | convolution fusion | flops 6727936000 | bytes 19026944 | tf_op jit(solution)/shard_map/dot_general | solution.py:104
  96.5 25.9 %all-gather.2.cloned.1.call-done = bf16[216,32,512]{2,1,0:T(8,128)(2,1)} async-done(((bf16[27,32,512]{2,1,0:T(8,128)(2,1)}), bf16[216,32,512]{2,1,0:T(8,128)(2,1)}) %all-gather.2.cloned.1.call-update) | async-done | bytes 7077904 | tf_op jit(solution)/shard_map/all_gather | solution.py:120
  122.3 10.9 %gather_fusion = bf16[137,32,512]{2,1,0:T(8,128)(2,1)} fusion(bf16[216,32,512]{2,1,0:T(8,128)(2,1)} %all-gather.2.cloned.1.call-done, s32[1024]{0:T(1024)S(1)} %pad_clamp_fusion.1), kind=kCustom, calls=%fused_computation | custom fusion | bytes 8978980 | tf_op jit(solution)/shard_map/jit(_take)/gather | solution.py:121
  142.7 6.1 %fusion.88 = (f32[2,1024]{1,0:T(2,128)S(1)}, f32[2,1024,512]{2,1,0:T(8,128)S(1)}) fusion(f32[512]{0:T(512)S(1)} %bitcast.134, f32[2,1030,512]{2,1,0:T(8,128)S(1)} %bitcast.114, f32[2,1024]{1,0:T(2,128)S(1)} %get-tuple-element.69, f32[512]{0:T(512)S(1)} %bitcast.136, f32[2,1024]{1,0:T(2,128)S(1)} %get-tuple-element.70, f32[512]{0:T(512)S(1)} %bitcast.138, ...), kind=kLoop, calls=%fused_computation.211 | loop fusion | flops 22018048 | bytes 33628160 | tf_op jit(solution)/shard_map/jvp()/reduce_sum | solution.py:86
  161.8 31.4 %multiply_convert_fusion = (bf16[2048,1536]{1,0:T(8,128)(2,1)S(1)}, f32[2048,1536]{1,0:T(8,128)}, f32[2048,1536]{1,0:T(8,128)}) fusion(f32[1536]{0:T(1024)S(1)} %reshape.280, bf16[2048,512]{1,0:T(8,128)(2,1)S(1)} %add_convert_fusion.3, bf16[1536,512]{1,0:T(8,128)(2,1)S(1)} %bitcast.123), kind=kOutput, calls=%fused_computation.6 | convolution fusion | flops 3428843520 | bytes 35133440 | tf_op jit(solution)/shard_map/dot_general | solution.py:104
  193.2 5.6 %fusion.86 = (f32[2048]{0:T(1024)S(1)}, f32[2048,512]{1,0:T(8,128)S(1)}, f32[2048,512]{1,0:T(8,128)}) fusion(f32[512]{0:T(512)S(1)} %bitcast.159, f32[512]{0:T(512)S(1)} %bitcast.157, bf16[2,1024,512]{2,1,0:T(8,128)(2,1)S(1)} %copy-done.16, bf16[2048,1536]{1,0:T(8,128)(2,1)S(1)} %get-tuple-element.32, bf16[1536,512]{1,0:T(8,128)(2,1)S(1)} %bitcast.125), kind=kOutput, calls=%fused_computation.210 | convolution fusion | flops 3226466304 | bytes 18362368 | tf_op jit(solution)/shard_map/dot_general | solution.py:104
  201.6 5.8 %convolution_add_fusion = f32[2048,1282]{0,1:T(8,128)S(1)} fusion(f32[1282]{0:T(1024)S(1)} %slice_convert_fusion.1, bf16[4384,512]{1,0:T(8,128)(2,1)} %copy-done.13, f32[2048,512]{1,0:T(8,128)} %copy-done.8, f32[512]{0:T(512)S(1)} %bitcast.169, f32[512]{0:T(512)S(1)} %bitcast.163, f32[2048]{0:T(1024)S(1)} %fusion.70, f32[2048]{0:T(1024)S(1)} %broadcast_multiply_fusion), kind=kOutput, calls=%fused_computation.22 | convolution fusion | flops 2696417280 | bytes 16040968 | tf_op jit(solution)/shard_map/dot_general | solution.py:104
  207.5 24.2 %add_convert_fusion.1 = (bf16[2048,641]{0,1:T(8,128)(2,1)S(1)}, bf16[2048,641]{0,1:T(8,128)(2,1)S(1)}, bf16[2048,641]{0,1:T(8,128)(2,1)}, bf16[2048,641]{0,1:T(8,128)(2,1)}) fusion(f32[2048,1282]{0,1:T(8,128)} %fusion.49, f32[2048,1282]{0,1:T(8,128)S(1)} %convolution_add_fusion), kind=kLoop, calls=%fused_computation.31 | loop fusion | flops 15753216 | bytes 31506432 | tf_op jit(solution)/shard_map/convert.2
  233.9 6.2 %multiply_reduce_fusion = (f32[512]{0:T(512)S(1)}, f32[2048]{0:T(1024)S(1)}, f32[512]{0:T(512)S(1)}, f32[2048,512]{1,0:T(8,128)S(1)}) fusion(f32[2048,512]{1,0:T(8,128)S(1)} %copy-done.9, f32[2048]{0:T(1024)S(1)} %fusion.70, f32[2048]{0:T(1024)S(1)} %broadcast_multiply_fusion, f32[512]{0:T(512)S(1)} %bitcast.164, bf16[4384,512]{1,0:T(8,128)(2,1)} %copy-done.13, ...), kind=kOutput, calls=%fused_computation.64 | convolution fusion | flops 2707436544 | bytes 14989312 | tf_op jit(solution)/shard_map/dot_general | solution.py:104
  253.1 16.6 %convert_reduce_fusion = (f32[1536]{0:T(1024)S(1)}, bf16[2048,1536]{1,0:T(8,128)(2,1)}) fusion(f32[2048,1536]{1,0:T(8,128)} %get-tuple-element.33, bf16[2048,512]{1,0:T(8,128)(2,1)} %copy-done.19, bf16[1536,512]{1,0:T(8,128)(2,1)} %bitcast.126, f32[2048,1536]{1,0:T(8,128)} %get-tuple-element.84, f32[1536]{0:T(1024)S(1)} %reshape.280), kind=kOutput, calls=%fused_computation.4 | convolution fusion | flops 3274701312 | bytes 35139584 | tf_op jit(solution)/shard_map/dot_general | solution.py:104
  269.7 6.7 %multiply_reduce_fusion.9 = (f32[2048]{0:T(1024)S(1)}, f32[2048,512]{1,0:T(8,128)S(1)}) fusion(f32[2048,512]{1,0:T(8,128)S(1)} %copy-done.4, f32[2048,512]{1,0:T(8,128)S(1)} %copy-done.6, bf16[2048,1536]{1,0:T(8,128)(2,1)} %get-tuple-element.90, bf16[1536,512]{1,0:T(8,128)(2,1)} %bitcast.124), kind=kOutput, calls=%fused_computation.76 | convolution fusion | flops 3224369152 | bytes 20455424 | tf_op jit(solution)/shard_map/dot_general | solution.py:104
  285.5 5.5 %fusion.84 = (f32[2048]{0:T(1024)S(1)}, f32[2048,512]{1,0:T(8,128)S(1)}) fusion(f32[2048]{0:T(1024)S(1)} %fusion.69, f32[2048]{0:T(1024)S(1)} %copy-done.39, f32[2048,512]{1,0:T(8,128)} %copy-done.7, f32[2048,512]{1,0:T(8,128)} %fusion.60, f32[2048]{0:T(1024)S(1)} %bitcast.132, f32[2,1024,512]{2,1,0:T(8,128)} %copy-done), kind=kLoop, calls=%fused_computation.208 | loop fusion | flops 7337984 | bytes 16809984 | tf_op jit(solution)/shard_map/transpose(jvp())/reduce_sum | solution.py:87
  300.1 27.2 %concatenate.42 = f32[4380,512]{1,0:T(8,128)} concatenate(f32[1536,512]{1,0:T(8,128)} %fusion.94, f32[1536,512]{1,0:T(8,128)S(1)} %fusion.95, f32[1282,512]{1,0:T(8,128)} %fusion.52, f32[1,512]{1,0:T(1,128)S(1)} %bitcast.156, f32[1,512]{1,0:T(1,128)S(1)} %bitcast.155, f32[1,512]{1,0:T(1,128)S(1)} %bitcast.154, f32[1,512]{1,0:T(1,128)S(1)} %bitcast.153, f32[1,512]{1,0:T(1,128)S(1)} %bitcast.152, ...), dimensions={0} | concatenate | bytes 17940480 | tf_op jit(solution)/shard_map/concatenate | solution.py:293
  327.2 8.1 %pad.35 = f32[4384,512]{1,0:T(8,128)} pad(f32[4380,512]{1,0:T(8,128)} %concatenate.42, f32[]{:T(128)} %constant.72.clone.1), padding=0_4x0_0 | pad | bytes 17948676 | tf_op jit(solution)/shard_map/jit(_pad)/pad | solution.py:296
  337.1 13.9 %fusion.6 = f32[2048,1280]{0,1:T(8,128)} fusion(bf16[2048,641]{0,1:T(8,128)(2,1)} %get-tuple-element.41, bf16[2048,641]{0,1:T(8,128)(2,1)S(1)} %copy-done.15, bf16[641,1280]{1,0:T(8,128)(2,1)} %get-tuple-element.91, bf16[641,1280]{1,0:T(8,128)(2,1)} %get-tuple-element.92), kind=kOutput, calls=%fused_computation.34 | convolution fusion | flops 6738438144 | bytes 19018752 | tf_op jit(solution)/shard_map/dot_general | solution.py:104
  350.9 14.4 %reshape.268 = f32[2,1024,4,320]{1,0,3,2:T(2,128)} reshape(f32[2048,1280]{0,1:T(8,128)} %fusion.6) | data formatting | bytes 20971520 | tf_op jit(solution)/shard_map/reshape | solution.py:189
  365.4 8.5 %copy_multiply_fusion = f32[2,1024,4,320]{1,3,0,2:T(8,128)S(1)} fusion(f32[2,1024,4,320]{1,0,3,2:T(2,128)} %reshape.268, f32[4,320]{1,0:T(4,128)S(1)} %copy-done.52), kind=kLoop, calls=%fused_computation.21 | loop fusion | flops 2621440 | bytes 20976640 | tf_op jit(solution)/shard_map/mul | solution.py:189
  396.1 20.3 %fusion.13 = f32[2,1024,512]{2,1,0:T(8,128)} fusion(f32[2,3,512]{2,1,0:T(4,128)S(1)} %collective-permute-done.5, f32[2,3,512]{2,1,0:T(4,128)S(1)} %collective-permute-done.4, f32[2,1024,512]{2,1,0:T(8,128)} %bitcast.119, f32[2,1024,512]{2,1,0:T(8,128)} %bitcast.118, f32[512]{0:T(512)S(1)} %bitcast.135, f32[2,1024]{1,0:T(2,128)S(1)} %copy-done.31, ...), kind=kLoop, calls=%fused_computation.46 | loop fusion | flops 27262976 | bytes 12670976 | tf_op jit(solution)/shard_map/add | solution.py:279
  416.3 103.8 %all-reduce.10.cloned.1.call-done = f32[137,32,512]{2,1,0:T(8,128)} async-done(((f32[137,32,512]{2,1,0:T(8,128)}), f32[137,32,512]{2,1,0:T(8,128)}) %all-reduce.10.cloned.1.call-update) | async-done | bytes 8978448 | tf_op jit(solution)/shard_map/psum | solution.py:298
  520.2 9.1 %concatenate.43 = f32[138,32,512]{2,1,0:T(8,128)} pad(f32[137,32,512]{2,1,0:T(8,128)} %all-reduce.10.cloned.1.call-done, f32[]{:T(128)} %constant.72.clone.1), padding=0_1x0_0x0_0 | pad | bytes 18022404 | tf_op jit(solution)/shard_map/concatenate | solution.py:299
  533.8 5.5 %multiply_subtract_fusion = (f32[27,32,512]{2,1,0:T(8,128)}, f32[27,32,512]{2,1,0:T(8,128)}, f32[27,32,512]{2,1,0:T(8,128)}) fusion(f32[27,32,512]{2,1,0:T(8,128)S(1)} %copy-done.12, f32[27,32,512]{2,1,0:T(8,128)S(1)} %gather_fusion.1, pred[27]{0:T(512)(128)(4,1)S(1)} %copy-done.68, f32[27,32,512]{2,1,0:T(8,128)} %param.13, f32[27,32,512]{2,1,0:T(8,128)} %param.14), kind=kLoop, calls=%fused_computation.127 | loop fusion | flops 7077888 | bytes 12386331 | tf_op jit(solution)/shard_map/sub | solution.py:306
  (260 shorter events, 130.7 us)
Async XLA Ops:
  7.2 115.2 %all-gather.2.cloned.1.call-start = ((), (), s32[]{:S(2)}) async-start(), calls=%async_computation | async-start | bytes 7962624 | tf_op jit(solution)/shard_map/all_gather | solution.py:120
  9.8 510.4 %all-reduce.10.cloned.1.call-start = ((), (), s32[]{:S(2)}) async-start(), calls=%async_computation.1 | async-start | bytes 17956864 | tf_op jit(solution)/shard_map/psum | solution.py:298
  10.6 41.3 %collective-permute-start = (bf16[2,3,512]{2,1,0:T(4,128)(2,1)S(1)}, bf16[2,3,512]{2,1,0:T(4,128)(2,1)S(1)}, u32[]{:S(2)}, u32[]{:S(2)}) collective-permute-start(bf16[2,3,512]{2,1,0:T(4,128)(2,1)S(1)} %get-tuple-element.55), channel_id=1, source_target_pairs={{0,1},{1,2},{2,3},{4,5},{5,6},{6,7},{8,9},{9,10},{10,11},{12,13},{... | collective-permute-start | bytes 18440 | tf_op jit(solution)/shard_map/ppermute | solution.py:36
  12.9 38.9 %collective-permute-start.1 = (bf16[2,3,512]{2,1,0:T(4,128)(2,1)S(1)}, bf16[2,3,512]{2,1,0:T(4,128)(2,1)S(1)}, u32[]{:S(2)}, u32[]{:S(2)}) collective-permute-start(bf16[2,3,512]{2,1,0:T(4,128)(2,1)S(1)} %get-tuple-element.54), channel_id=1, source_target_pairs={{1,0},{2,1},{3,2},{5,4},{6,5},{7,6},{9,8},{10,9},{11,10},{13,12},{... | collective-permute-start | bytes 18440 | tf_op jit(solution)/shard_map/ppermute | solution.py:39
  20.9 12.1 %copy-start.50 = (f32[320]{0:T(512)}, f32[320]{0:T(512)S(1)}, u32[]{:S(2)}) copy-start(f32[320]{0:T(512)S(1)} %get-tuple-element.78) | copy-start | bytes 3844
  21.1 119.1 %copy-start.24 = (f32[2,1024]{1,0:T(2,128)}, f32[2,1024]{1,0:T(2,128)S(1)}, u32[]{:S(2)}) copy-start(f32[2,1024]{1,0:T(2,128)S(1)} %get-tuple-element.68) | copy-start | bytes 24580
  21.1 119.1 %copy-start.26 = (f32[2,1024]{1,0:T(2,128)}, f32[2,1024]{1,0:T(2,128)S(1)}, u32[]{:S(2)}) copy-start(f32[2,1024]{1,0:T(2,128)S(1)} %get-tuple-element.72) | copy-start | bytes 24580
  21.1 119.1 %copy-start.28 = (f32[2,1024]{1,0:T(2,128)}, f32[2,1024]{1,0:T(2,128)S(1)}, u32[]{:S(2)}) copy-start(f32[2,1024]{1,0:T(2,128)S(1)} %get-tuple-element.73) | copy-start | bytes 24580
  21.1 119.1 %copy-start.30 = (f32[2,1024]{1,0:T(2,128)}, f32[2,1024]{1,0:T(2,128)S(1)}, u32[]{:S(2)}) copy-start(f32[2,1024]{1,0:T(2,128)S(1)} %get-tuple-element.69) | copy-start | bytes 24580
  21.1 119.1 %copy-start.32 = (f32[2,1024]{1,0:T(2,128)}, f32[2,1024]{1,0:T(2,128)S(1)}, u32[]{:S(2)}) copy-start(f32[2,1024]{1,0:T(2,128)S(1)} %get-tuple-element.70) | copy-start | bytes 24580
  21.1 119.1 %copy-start.34 = (f32[2,1024]{1,0:T(2,128)}, f32[2,1024]{1,0:T(2,128)S(1)}, u32[]{:S(2)}) copy-start(f32[2,1024]{1,0:T(2,128)S(1)} %get-tuple-element.71) | copy-start | bytes 24580
  24.8 39.0 %collective-permute-start.3 = (f32[2,3,320]{1,2,0:T(8,128)}, f32[2,3,320]{1,2,0:T(8,128)}, u32[]{:S(2)}, u32[]{:S(2)}) collective-permute-start(f32[2,3,320]{1,2,0:T(8,128)} %slice.387), channel_id=1, source_target_pairs={{1,0},{2,1},{3,2},{5,4},{6,5},{7,6},{9,8},{10,9},{11,10},{13,12},{... | collective-permute-start | bytes 23048 | tf_op jit(solution)/shard_map/ppermute | solution.py:47
  51.8 105.1 %copy-start.36 = (s32[1,8,2,128]{3,1,2,0:T(8,128)}, s32[1,8,2,128]{3,1,2,0:T(8,128)S(1)}, u32[]{:S(2)}) copy-start(s32[1,8,2,128]{3,1,2,0:T(8,128)S(1)} %copy.53) | copy-start | bytes 24580
  137.4 14.7 %copy-start.13 = (bf16[4384,512]{1,0:T(8,128)(2,1)}, bf16[4384,512]{1,0:T(8,128)(2,1)S(1)}, u32[]{:S(2)}) copy-start(bf16[4384,512]{1,0:T(8,128)(2,1)S(1)} %bitcast_select_fusion) | copy-start | bytes 13467652
  157.8 35.4 %copy-start.23 = (bf16[48,32,512]{2,1,0:T(8,128)(2,1)}, bf16[48,32,512]{2,1,0:T(8,128)(2,1)S(1)}, u32[]{:S(2)}) copy-start(bf16[48,32,512]{2,1,0:T(8,128)(2,1)S(1)} %get-tuple-element.45) | copy-start | bytes 4718596
  161.8 31.4 %copy-start.17 = (bf16[2048,512]{1,0:T(8,128)(2,1)}, bf16[2048,512]{1,0:T(8,128)(2,1)S(1)}, u32[]{:S(2)}) copy-start(bf16[2048,512]{1,0:T(8,128)(2,1)S(1)} %add_convert_fusion.3) | copy-start | bytes 6291460
  161.8 31.4 %copy-start.16 = (bf16[2,1024,512]{2,1,0:T(8,128)(2,1)S(1)}, bf16[2,1024,512]{2,1,0:T(8,128)(2,1)}, u32[]{:S(2)}) copy-start(bf16[2,1024,512]{2,1,0:T(8,128)(2,1)} %param.8) | copy-start | bytes 6291460
  253.1 16.6 %copy-start.4 = (f32[2048,512]{1,0:T(8,128)S(1)}, f32[2048,512]{1,0:T(8,128)}, u32[]{:S(2)}) copy-start(f32[2048,512]{1,0:T(8,128)} %bitcast_subtract_fusion) | copy-start | bytes 12582916
  253.1 16.6 %copy-start.6 = (f32[2048,512]{1,0:T(8,128)S(1)}, f32[2048,512]{1,0:T(8,128)}, u32[]{:S(2)}) copy-start(f32[2048,512]{1,0:T(8,128)} %fusion.60) | copy-start | bytes 12582916
  350.9 14.4 %copy-start.52 = (f32[4,320]{1,0:T(4,128)S(1)}, f32[4,320]{1,0:T(4,128)}, u32[]{:S(2)}) copy-start(f32[4,320]{1,0:T(4,128)} %multiply_subtract_fusion.2) | copy-start | bytes 15364
  376.4 10.3 %collective-permute-start.2 = (f32[2,3,320]{1,2,0:T(8,128)S(1)}, f32[2,3,320]{1,2,0:T(8,128)S(1)}, u32[]{:S(2)}, u32[]{:S(2)}) collective-permute-start(f32[2,3,320]{1,2,0:T(8,128)S(1)} %pad_add_fusion.1), channel_id=1, source_target_pairs={{0,1},{1,2},{2,3},{4,5},{5,6},{6,7},{8,9},{9,10},{10,11},{12,13},{... | collective-permute-start | bytes 23048 | tf_op jit(solution)/shard_map/ppermute | solution.py:47
  381.1 14.9 %collective-permute-start.4 = (f32[2,3,512]{2,1,0:T(4,128)S(1)}, f32[2,3,512]{2,1,0:T(4,128)S(1)}, u32[]{:S(2)}, u32[]{:S(2)}) collective-permute-start(f32[2,3,512]{2,1,0:T(4,128)S(1)} %get-tuple-element.49), channel_id=1, source_target_pairs={{1,0},{2,1},{3,2},{5,4},{6,5},{7,6},{9,8},{10,9},{11,10},{13,12},{... | collective-permute-start | bytes 36872 | tf_op jit(solution)/shard_map/ppermute | solution.py:39
  382.3 13.6 %collective-permute-start.5 = (f32[2,3,512]{2,1,0:T(4,128)S(1)}, f32[2,3,512]{2,1,0:T(4,128)S(1)}, u32[]{:S(2)}, u32[]{:S(2)}) collective-permute-start(f32[2,3,512]{2,1,0:T(4,128)S(1)} %get-tuple-element.50), channel_id=1, source_target_pairs={{0,1},{1,2},{2,3},{4,5},{5,6},{6,7},{8,9},{9,10},{10,11},{12,13},{... | collective-permute-start | bytes 36872 | tf_op jit(solution)/shard_map/ppermute | solution.py:36
  416.3 117.4 %copy-start.68 = (pred[27]{0:T(512)(128)(4,1)S(1)}, pred[27]{0:T(512)(128)(4,1)}, u32[]{:S(2)}) copy-start(pred[27]{0:T(512)(128)(4,1)} %get-tuple-element.18) | copy-start | bytes 85
  (62 other events, 337.7 us)
Sparse Core Ops, SparseCore 0:
  10.8 111.5 all-gather.1
  335.5 184.6 all-reduce.9
where the time goes:
time: 556 us; the launch traced here: 546 us
  other arithmetic  136 us (24%)
  local copies, waits for them, and re-layouts  133 us (24%)
  waiting for transfers between devices  130 us (23%)
  matrix products  119 us (21%)
  between operations  15.7 us (3%)
  starting transfers between devices  12.2 us (2%)
    dot_general x11, matrix products, contract(): lax.dot_general(left_side, right_side, (((left_dim,), (right_dim,)), ((),...  109 us
    psum x1, waiting for transfers between devices, local(): summed = lax.psum(grad_buckets, ('rows', 'seq'))  104 us
    another operation x3, other arithmetic  42.2 us
    concatenate x1, local copies, waits for them, and re-layouts, local(): jnp.concatenate([grad_w_in, grad_w_out, grad_w_head, vec_grads, in_rows,...  27.2 us
    all_gather x1, waiting for transfers between devices, local(): lax.all_gather(master.astype(jnp.bfloat16), 'rows', axis=0, tiled=True)  25.9 us
    add x1, other arithmetic, local(): input_grad + conv_weight[tap_index] * keep * halo_grad[:, begin:begin + f...  20.3 us
    unnamed x159, local copies, waits for them, and re-layouts  17.5 us
    reshape x1, local copies, waits for them, and re-layouts, local(): signal.reshape(rows_here, frames_here, lap_count, HOP)  14.4 us
  transfers between devices with their start and end apart: 8, of which 2 were waited for; matrix products, arithmetic and copies ran while one was open for 28% of the time, Pallas kernels for 0%

commit v1 on v0

--- a/solution.py
+++ b/solution.py
@@ -28,6 +28,27 @@
 ADAM_EPS = 1e-08
 
 
+def gather_around(value, axis, dim):
+    size, index, rows = (lax.axis_size(axis), lax.axis_index(axis), value.shape[dim])
+    ahead = [(i, (i + 1) % size) for i in range(size)]
+    left = [(i, (i - 1) % size) for i in range(size)]
+    result = jnp.zeros((*value.shape[:dim], size * rows, *value.shape[dim + 1 :]), value.dtype)
+    result = lax.dynamic_update_slice_in_dim(result, value, index * rows, axis=dim)
+    from_left = from_right = value
+    halfway = size // 2
+    for hop in range(1, halfway + 1):
+        from_left = lax.ppermute(from_left, axis, ahead)
+        result = lax.dynamic_update_slice_in_dim(
+            result, from_left, (index - hop) % size * rows, axis=dim
+        )
+        if hop < size - halfway:
+            from_right = lax.ppermute(from_right, axis, left)
+            result = lax.dynamic_update_slice_in_dim(
+                result, from_right, (index + hop) % size * rows, axis=dim
+            )
+    return result
+
+
 def padded(block, sides, width):
     for axis, dim in sides:
         count = lax.axis_size(axis)
@@ -117,7 +138,7 @@
     rim_width = (KW - 1) // 2
     margin = max(rim_width, lap_count - 1)
     bucket_place, source = slot_maps(owner_list, lax.axis_size("rows"), slot_count)
-    gathered = lax.all_gather(master.astype(jnp.bfloat16), "rows", axis=0, tiled=True)
+    gathered = gather_around(master.astype(jnp.bfloat16), "rows", 0)
     buckets = jnp.take(gathered, bucket_place, axis=0)
     weight_table = buckets.reshape(-1, channels)[:PR]
     w_in = weight_table[:FF]

time: 556 us -> 597 us (1.074)
  waiting for transfers between devices: 130 us -> 149 us
  starting transfers between devices: 12.2 us -> 26.4 us
  local copies, waits for them, and re-layouts: 133 us -> 143 us
    ppermute x0 -> x7, waiting for transfers between devices: none -> 41.7 us  [the longest x3 30.6 us: gather_around(): from_right = lax.ppermute(from_right, axis, left)]
    all_gather x1 -> x0, waiting for transfers between devices: 25.9 us -> none  [local(): lax.all_gather(master.astype(jnp.bfloat16), 'rows', axis=0, tiled=True)]
    ppermute x0 -> x7, starting transfers between devices: none -> 14.8 us  [the longest x3 8.78 us: gather_around(): from_right = lax.ppermute(from_right, axis, left)]
    dynamic_update_slice x0 -> x7, local copies, waits for them, and re-layouts: none -> 10.5 us  [the longest x4 6.35 us: gather_around(): lax.dynamic_update_slice_in_dim(result, from_left, (index - hop) % size *...]
    unnamed x159 -> x163, local copies, waits for them, and re-layouts: 17.5 us -> 15.5 us
  transfers between devices with their start and end apart: 8 -> 14, of which waited for: 2 -> 4; matrix products, arithmetic and copies ran while one was open for 28% -> 28% of each run, Pallas kernels for 0% -> 0%
where the time goes in v1:
time: 597 us; the launch traced here: 589 us
  waiting for transfers between devices  149 us (25%)
  local copies, waits for them, and re-layouts  143 us (24%)
  other arithmetic  134 us (22%)
  matrix products  120 us (20%)
  starting transfers between devices  26.4 us (4%)
  between operations  16 us (3%)
    dot_general x11, matrix products, contract(): lax.dot_general(left_side, right_side, (((left_dim,), (right_dim,)), ((),...  108 us
    psum x1, waiting for transfers between devices, local(): summed = lax.psum(grad_buckets, ('rows', 'seq'))  108 us
    another operation x3, other arithmetic  42.4 us
    ppermute x3, waiting for transfers between devices, gather_around(): from_right = lax.ppermute(from_right, axis, left)  30.6 us
    concatenate x1, local copies, waits for them, and re-layouts, local(): jnp.concatenate([grad_w_in, grad_w_out, grad_w_head, vec_grads, in_rows,...  27.2 us
    add x1, other arithmetic, local(): input_grad + conv_weight[tap_index] * keep * halo_grad[:, begin:begin + f...  20.7 us
    unnamed x163, local copies, waits for them, and re-layouts  15.5 us
    reshape x1, local copies, waits for them, and re-layouts, local(): signal.reshape(rows_here, frames_here, lap_count, HOP)  14.4 us
  transfers between devices with their start and end apart: 14, of which 4 were waited for; matrix products, arithmetic and copies ran while one was open for 28% of the time, Pallas kernels for 0%

profile of v1, /device:TPU:0, one launch (start us, length us, event | category | flops | bytes accessed | tf_op | source)
XLA Modules:
  0.0 588.6 jit_solution(11173948216280326282)
XLA Ops:
  42.4 11.1 %collective-permute-done = bf16[27,32,512]{2,1,0:T(8,128)(2,1)} collective-permute-done((bf16[27,32,512]{2,1,0:T(8,128)(2,1)}, bf16[27,32,512]{2,1,0:T(8,128)(2,1)}, u32[]{:S(2)}, u32[]{:S(2)}) %collective-permute-start) | collective-permute-done | bytes 884768 | tf_op jit(solution)/shard_map/ppermute | solution.py:40
  57.5 15.2 %multiply_convert_fusion.2 = (bf16[641,1280]{1,0:T(8,128)(2,1)}, bf16[641,1280]{1,0:T(8,128)(2,1)}) fusion(f32[641]{0:T(1024)S(1)} %fusion.74, f32[641]{0:T(1024)S(1)} %select_multiply_fusion), kind=kLoop, calls=%fused_computation.89 | loop fusion | flops 10666240 | bytes 3287048 | tf_op jit(solution)/shard_map/convert.12
  73.5 9.3 %concatenate.35 = bf16[2,1030,512]{2,1,0:T(8,128)(2,1)S(1)} concatenate(bf16[2,3,512]{2,1,0:T(4,128)(2,1)S(1)} %collective-permute-done.7, bf16[2,1024,512]{2,1,0:T(8,128)(2,1)} %param.8, bf16[2,3,512]{2,1,0:T(4,128)(2,1)S(1)} %collective-permute-done.8), dimensions={1} | concatenate | bytes 4218880 | tf_op jit(solution)/shard_map/concatenate | solution.py:61
  96.4 10.2 %copy.34 = bf16[2,1024,4,320]{1,0,3,2:T(2,128)(2,1)} copy(bf16[2,1024,4,320]{1,3,0,2:T(8,128)(2,1)} %pad_maximum_fusion.1) | data formatting | bytes 10485760 | tf_op jit(solution)/shard_map/stack | solution.py:237
  111.4 13.5 %collective-permute-done.3 = bf16[27,32,512]{2,1,0:T(8,128)(2,1)S(1)} collective-permute-done((bf16[27,32,512]{2,1,0:T(8,128)(2,1)}, bf16[27,32,512]{2,1,0:T(8,128)(2,1)S(1)}, u32[]{:S(2)}, u32[]{:S(2)}) %collective-permute-start.3) | collective-permute-done | bytes 884768 | tf_op jit(solution)/shard_map/ppermute | solution.py:45
  128.0 9.6 %fusion.49 = f32[2048,1282]{0,1:T(8,128)} fusion(bf16[2048,1280]{0,1:T(8,128)(2,1)S(1)} %bitcast.122, bf16[641,1280]{1,0:T(8,128)(2,1)S(1)} %copy-done.20, bf16[641,1280]{1,0:T(8,128)(2,1)S(1)} %copy-done.21), kind=kOutput, calls=%fused_computation.122 | convolution fusion | flops 6727936000 | bytes 19026944 | tf_op jit(solution)/shard_map/dot_general | solution.py:125
  146.1 17.1 %collective-permute-done.5 = bf16[27,32,512]{2,1,0:T(8,128)(2,1)S(1)} collective-permute-done((bf16[27,32,512]{2,1,0:T(8,128)(2,1)S(1)}, bf16[27,32,512]{2,1,0:T(8,128)(2,1)S(1)}, u32[]{:S(2)}, u32[]{:S(2)}) %collective-permute-start.5) | collective-permute-done | bytes 884768 | tf_op jit(solution)/shard_map/ppermute | solution.py:45
  165.1 10.5 %gather_fusion = bf16[137,32,512]{2,1,0:T(8,128)(2,1)} fusion(bf16[216,32,512]{2,1,0:T(8,128)(2,1)} %constant_dynamic-update-slice_fusion, s32[1024]{0:T(1024)S(1)} %pad_clamp_fusion.1), kind=kCustom, calls=%fused_computation | custom fusion | bytes 8978980 | tf_op jit(solution)/shard_map/jit(_take)/gather | solution.py:142
  181.8 6.1 %fusion.88 = (f32[2,1024]{1,0:T(2,128)S(1)}, f32[2,1024,512]{2,1,0:T(8,128)S(1)}) fusion(f32[512]{0:T(512)S(1)} %bitcast.134, f32[2,1030,512]{2,1,0:T(8,128)S(1)} %bitcast.114, f32[2,1024]{1,0:T(2,128)S(1)} %get-tuple-element.71, f32[512]{0:T(512)S(1)} %bitcast.136, f32[2,1024]{1,0:T(2,128)S(1)} %get-tuple-element.72, f32[512]{0:T(512)S(1)} %bitcast.138, ...), kind=kLoop, calls=%fused_computation.219 | loop fusion | flops 22018048 | bytes 33628160 | tf_op jit(solution)/shard_map/jvp()/reduce_sum | solution.py:107
  200.1 31.6 %multiply_convert_fusion = (bf16[2048,1536]{1,0:T(8,128)(2,1)S(1)}, f32[2048,1536]{1,0:T(8,128)}, f32[2048,1536]{1,0:T(8,128)}) fusion(f32[1536]{0:T(1024)S(1)} %reshape.280, bf16[2048,512]{1,0:T(8,128)(2,1)S(1)} %add_convert_fusion.3, bf16[1536,512]{1,0:T(8,128)(2,1)S(1)} %bitcast.123), kind=kOutput, calls=%fused_computation.6 | convolution fusion | flops 3428843520 | bytes 35133440 | tf_op jit(solution)/shard_map/dot_general | solution.py:125
  240.0 5.8 convolution_add_fusion
  245.9 24.4 %add_convert_fusion.1 = (bf16[2048,641]{0,1:T(8,128)(2,1)S(1)}, bf16[2048,641]{0,1:T(8,128)(2,1)S(1)}, bf16[2048,641]{0,1:T(8,128)(2,1)}, bf16[2048,641]{0,1:T(8,128)(2,1)}) fusion(f32[2048,1282]{0,1:T(8,128)} %fusion.49, f32[2048,1282]{0,1:T(8,128)S(1)} %convolution_add_fusion), kind=kLoop, calls=%fused_computation.31 | loop fusion | flops 15753216 | bytes 31506432 | tf_op jit(solution)/shard_map/convert.2
  272.5 6.2 %multiply_reduce_fusion = (f32[512]{0:T(512)S(1)}, f32[2048]{0:T(1024)S(1)}, f32[512]{0:T(512)S(1)}, f32[2048,512]{1,0:T(8,128)S(1)}) fusion(f32[2048,512]{1,0:T(8,128)S(1)} %copy-done.8, f32[2048]{0:T(1024)S(1)} %fusion.70, f32[2048]{0:T(1024)S(1)} %broadcast_multiply_fusion, f32[512]{0:T(512)S(1)} %bitcast.164, bf16[4384,512]{1,0:T(8,128)(2,1)} %copy-done.13, ...), kind=kOutput, calls=%fused_computation.64 | convolution fusion | flops 2707436544 | bytes 14989312 | tf_op jit(solution)/shard_map/dot_general | solution.py:125
  291.5 16.5 %convert_reduce_fusion = (f32[1536]{0:T(1024)S(1)}, bf16[2048,1536]{1,0:T(8,128)(2,1)}) fusion(f32[2048,1536]{1,0:T(8,128)} %get-tuple-element.33, bf16[2048,512]{1,0:T(8,128)(2,1)} %copy-done.19, bf16[1536,512]{1,0:T(8,128)(2,1)} %bitcast.126, f32[2048,1536]{1,0:T(8,128)} %get-tuple-element.86, f32[1536]{0:T(1024)S(1)} %reshape.280), kind=kOutput, calls=%fused_computation.4 | convolution fusion | flops 3274701312 | bytes 35139584 | tf_op jit(solution)/shard_map/dot_general | solution.py:125
  308.0 6.4 %multiply_reduce_fusion.9 = (f32[2048]{0:T(1024)S(1)}, f32[2048,512]{1,0:T(8,128)S(1)}) fusion(f32[2048,512]{1,0:T(8,128)S(1)} %copy-done.3, f32[2048,512]{1,0:T(8,128)S(1)} %copy-done.5, bf16[2048,1536]{1,0:T(8,128)(2,1)} %get-tuple-element.92, bf16[1536,512]{1,0:T(8,128)(2,1)} %bitcast.124), kind=kOutput, calls=%fused_computation.76 | convolution fusion | flops 3224369152 | bytes 20455424 | tf_op jit(solution)/shard_map/dot_general | solution.py:125
  323.5 5.5 fusion.84
  338.1 27.2 %concatenate.42 = f32[4380,512]{1,0:T(8,128)} concatenate(f32[1536,512]{1,0:T(8,128)} %fusion.94, f32[1536,512]{1,0:T(8,128)S(1)} %fusion.95, f32[1282,512]{1,0:T(8,128)} %fusion.52, f32[1,512]{1,0:T(1,128)S(1)} %bitcast.156, f32[1,512]{1,0:T(1,128)S(1)} %bitcast.155, f32[1,512]{1,0:T(1,128)S(1)} %bitcast.154, f32[1,512]{1,0:T(1,128)S(1)} %bitcast.153, f32[1,512]{1,0:T(1,128)S(1)} %bitcast.152, ...), dimensions={0} | concatenate | bytes 17940480 | tf_op jit(solution)/shard_map/concatenate | solution.py:314
  365.4 8.1 %pad.35 = f32[4384,512]{1,0:T(8,128)} pad(f32[4380,512]{1,0:T(8,128)} %concatenate.42, f32[]{:T(128)} %constant.186.clone.1), padding=0_4x0_0 | pad | bytes 17948676 | tf_op jit(solution)/shard_map/jit(_pad)/pad | solution.py:317
  375.2 13.5 %fusion.6 = f32[2048,1280]{0,1:T(8,128)} fusion(bf16[2048,641]{0,1:T(8,128)(2,1)} %get-tuple-element.43, bf16[2048,641]{0,1:T(8,128)(2,1)S(1)} %copy-done.15, bf16[641,1280]{1,0:T(8,128)(2,1)} %get-tuple-element.93, bf16[641,1280]{1,0:T(8,128)(2,1)} %get-tuple-element.94), kind=kOutput, calls=%fused_computation.34 | convolution fusion | flops 6738438144 | bytes 19018752 | tf_op jit(solution)/shard_map/dot_general | solution.py:125
  388.7 14.4 %reshape.268 = f32[2,1024,4,320]{1,0,3,2:T(2,128)} reshape(f32[2048,1280]{0,1:T(8,128)} %fusion.6) | data formatting | bytes 20971520 | tf_op jit(solution)/shard_map/reshape | solution.py:210
  403.2 8.6 %copy_multiply_fusion = f32[2,1024,4,320]{1,3,0,2:T(8,128)S(1)} fusion(f32[2,1024,4,320]{1,0,3,2:T(2,128)} %reshape.268, f32[4,320]{1,0:T(4,128)S(1)} %copy-done.52), kind=kLoop, calls=%fused_computation.21 | loop fusion | flops 2621440 | bytes 20976640 | tf_op jit(solution)/shard_map/mul | solution.py:210
  434.0 20.7 %fusion.13 = f32[2,1024,512]{2,1,0:T(8,128)} fusion(f32[2,3,512]{2,1,0:T(4,128)S(1)} %collective-permute-done.12, f32[2,3,512]{2,1,0:T(4,128)S(1)} %collective-permute-done.11, f32[2,1024,512]{2,1,0:T(8,128)} %bitcast.119, f32[2,1024,512]{2,1,0:T(8,128)} %bitcast.118, f32[512]{0:T(512)S(1)} %bitcast.135, f32[2,1024]{1,0:T(2,128)S(1)} %copy-done.31, ...), kind=kLoop, calls=%fused_computation.46 | loop fusion | flops 27262976 | bytes 12670976 | tf_op jit(solution)/shard_map/add | solution.py:300
  454.6 107.6 %all-reduce.10.cloned.1.call-done = f32[137,32,512]{2,1,0:T(8,128)} async-done(((f32[137,32,512]{2,1,0:T(8,128)}), f32[137,32,512]{2,1,0:T(8,128)}) %all-reduce.10.cloned.1.call-update) | async-done | bytes 8978448 | tf_op jit(solution)/shard_map/psum | solution.py:319
  562.2 9.1 %concatenate.43 = f32[138,32,512]{2,1,0:T(8,128)} pad(f32[137,32,512]{2,1,0:T(8,128)} %all-reduce.10.cloned.1.call-done, f32[]{:T(128)} %constant.186.clone.1), padding=0_1x0_0x0_0 | pad | bytes 18022404 | tf_op jit(solution)/shard_map/concatenate | solution.py:320
  (283 shorter events, 164.5 us)
Async XLA Ops:
  7.2 555.0 %all-reduce.10.cloned.1.call-start = ((), (), s32[]{:S(2)}) async-start(), calls=%async_computation | async-start | bytes 17956864 | tf_op jit(solution)/shard_map/psum | solution.py:319
  12.5 41.1 %collective-permute-start = (bf16[27,32,512]{2,1,0:T(8,128)(2,1)}, bf16[27,32,512]{2,1,0:T(8,128)(2,1)}, u32[]{:S(2)}, u32[]{:S(2)}) collective-permute-start(bf16[27,32,512]{2,1,0:T(8,128)(2,1)} %get-tuple-element.39), channel_id=1, source_target_pairs={{0,4},{4,8},{8,12},{12,16},{16,20},{20,24},{24,28},{28,0},{1,5},{5... | collective-permute-start | bytes 2654216 | tf_op jit(solution)/shard_map/ppermute | solution.py:40
  15.4 70.1 %collective-permute-start.1 = (bf16[27,32,512]{2,1,0:T(8,128)(2,1)}, bf16[27,32,512]{2,1,0:T(8,128)(2,1)}, u32[]{:S(2)}, u32[]{:S(2)}) collective-permute-start(bf16[27,32,512]{2,1,0:T(8,128)(2,1)} %get-tuple-element.39), channel_id=1, source_target_pairs={{0,28},{4,0},{8,4},{12,8},{16,12},{20,16},{24,20},{28,24},{1,29},{... | collective-permute-start | bytes 2654216 | tf_op jit(solution)/shard_map/ppermute | solution.py:45
  19.8 53.8 %collective-permute-start.7 = (bf16[2,3,512]{2,1,0:T(4,128)(2,1)}, bf16[2,3,512]{2,1,0:T(4,128)(2,1)S(1)}, u32[]{:S(2)}, u32[]{:S(2)}) collective-permute-start(bf16[2,3,512]{2,1,0:T(4,128)(2,1)} %get-tuple-element.57), channel_id=1, source_target_pairs={{0,1},{1,2},{2,3},{4,5},{5,6},{6,7},{8,9},{9,10},{10,11},{12,13},{... | collective-permute-start | bytes 18440 | tf_op jit(solution)/shard_map/ppermute | solution.py:57
  21.2 52.3 %collective-permute-start.8 = (bf16[2,3,512]{2,1,0:T(4,128)(2,1)S(1)}, bf16[2,3,512]{2,1,0:T(4,128)(2,1)S(1)}, u32[]{:S(2)}, u32[]{:S(2)}) collective-permute-start(bf16[2,3,512]{2,1,0:T(4,128)(2,1)S(1)} %get-tuple-element.56), channel_id=1, source_target_pairs={{1,0},{2,1},{3,2},{5,4},{6,5},{7,6},{9,8},{10,9},{11,10},{13,12},{... | collective-permute-start | bytes 18440 | tf_op jit(solution)/shard_map/ppermute | solution.py:60
  23.0 158.7 %copy-start.24 = (f32[2,1024]{1,0:T(2,128)}, f32[2,1024]{1,0:T(2,128)S(1)}, u32[]{:S(2)}) copy-start(f32[2,1024]{1,0:T(2,128)S(1)} %get-tuple-element.70) | copy-start | bytes 24580
  23.0 158.7 %copy-start.26 = (f32[2,1024]{1,0:T(2,128)}, f32[2,1024]{1,0:T(2,128)S(1)}, u32[]{:S(2)}) copy-start(f32[2,1024]{1,0:T(2,128)S(1)} %get-tuple-element.74) | copy-start | bytes 24580
  23.1 158.7 %copy-start.28 = (f32[2,1024]{1,0:T(2,128)}, f32[2,1024]{1,0:T(2,128)S(1)}, u32[]{:S(2)}) copy-start(f32[2,1024]{1,0:T(2,128)S(1)} %get-tuple-element.75) | copy-start | bytes 24580
  23.1 158.7 %copy-start.30 = (f32[2,1024]{1,0:T(2,128)}, f32[2,1024]{1,0:T(2,128)S(1)}, u32[]{:S(2)}) copy-start(f32[2,1024]{1,0:T(2,128)S(1)} %get-tuple-element.71) | copy-start | bytes 24580
  23.1 158.7 %copy-start.32 = (f32[2,1024]{1,0:T(2,128)}, f32[2,1024]{1,0:T(2,128)S(1)}, u32[]{:S(2)}) copy-start(f32[2,1024]{1,0:T(2,128)S(1)} %get-tuple-element.72) | copy-start | bytes 24580
  23.1 158.7 %copy-start.34 = (f32[2,1024]{1,0:T(2,128)}, f32[2,1024]{1,0:T(2,128)S(1)}, u32[]{:S(2)}) copy-start(f32[2,1024]{1,0:T(2,128)S(1)} %get-tuple-element.73) | copy-start | bytes 24580
  31.7 57.1 %collective-permute-start.10 = (f32[2,3,320]{1,2,0:T(8,128)}, f32[2,3,320]{1,2,0:T(8,128)}, u32[]{:S(2)}, u32[]{:S(2)}) collective-permute-start(f32[2,3,320]{1,2,0:T(8,128)} %slice.387), channel_id=1, source_target_pairs={{1,0},{2,1},{3,2},{5,4},{6,5},{7,6},{9,8},{10,9},{11,10},{13,12},{... | collective-permute-start | bytes 23048 | tf_op jit(solution)/shard_map/ppermute | solution.py:68
  39.4 33.8 %copy-start.68 = (pred[137]{0:T(512)(128)(4,1)S(1)}, pred[137]{0:T(512)(128)(4,1)}, u32[]{:S(2)}) copy-start(pred[137]{0:T(512)(128)(4,1)} %get-tuple-element.36) | copy-start | bytes 415
  53.6 34.9 %collective-permute-start.2 = (bf16[27,32,512]{2,1,0:T(8,128)(2,1)}, bf16[27,32,512]{2,1,0:T(8,128)(2,1)}, u32[]{:S(2)}, u32[]{:S(2)}) collective-permute-start(bf16[27,32,512]{2,1,0:T(8,128)(2,1)} %collective-permute-done), channel_id=1, source_target_pairs={{0,4},{4,8},{8,12},{12,16},{16,20},{20,24},{24,28},{28,0},{1,5},{5... | collective-permute-start | bytes 2654216 | tf_op jit(solution)/shard_map/ppermute | solution.py:40
  73.5 121.5 %copy-start.36 = (s32[1,8,2,128]{3,1,2,0:T(8,128)}, s32[1,8,2,128]{3,1,2,0:T(8,128)S(1)}, u32[]{:S(2)}) copy-start(s32[1,8,2,128]{3,1,2,0:T(8,128)S(1)} %copy.47) | copy-start | bytes 24580
  85.5 39.4 %collective-permute-start.3 = (bf16[27,32,512]{2,1,0:T(8,128)(2,1)}, bf16[27,32,512]{2,1,0:T(8,128)(2,1)S(1)}, u32[]{:S(2)}, u32[]{:S(2)}) collective-permute-start(bf16[27,32,512]{2,1,0:T(8,128)(2,1)} %collective-permute-done.1), channel_id=1, source_target_pairs={{0,28},{4,0},{8,4},{12,8},{16,12},{20,16},{24,20},{28,24},{1,29},{... | collective-permute-start | bytes 2654216 | tf_op jit(solution)/shard_map/ppermute | solution.py:45
  88.5 39.1 %collective-permute-start.4 = (bf16[27,32,512]{2,1,0:T(8,128)(2,1)}, bf16[27,32,512]{2,1,0:T(8,128)(2,1)S(1)}, u32[]{:S(2)}, u32[]{:S(2)}) collective-permute-start(bf16[27,32,512]{2,1,0:T(8,128)(2,1)} %collective-permute-done.2), channel_id=1, source_target_pairs={{0,4},{4,8},{8,12},{12,16},{16,20},{20,24},{24,28},{28,0},{1,5},{5... | collective-permute-start | bytes 2654216 | tf_op jit(solution)/shard_map/ppermute | solution.py:40
  124.9 38.3 %collective-permute-start.5 = (bf16[27,32,512]{2,1,0:T(8,128)(2,1)S(1)}, bf16[27,32,512]{2,1,0:T(8,128)(2,1)S(1)}, u32[]{:S(2)}, u32[]{:S(2)}) collective-permute-start(bf16[27,32,512]{2,1,0:T(8,128)(2,1)S(1)} %collective-permute-done.3), channel_id=1, source_target_pairs={{0,28},{4,0},{8,4},{12,8},{16,12},{20,16},{24,20},{28,24},{1,29},{... | collective-permute-start | bytes 2654216 | tf_op jit(solution)/shard_map/ppermute | solution.py:45
  127.6 36.6 %collective-permute-start.6 = (bf16[27,32,512]{2,1,0:T(8,128)(2,1)S(1)}, bf16[27,32,512]{2,1,0:T(8,128)(2,1)S(1)}, u32[]{:S(2)}, u32[]{:S(2)}) collective-permute-start(bf16[27,32,512]{2,1,0:T(8,128)(2,1)S(1)} %collective-permute-done.4), channel_id=1, source_target_pairs={{0,4},{4,8},{8,12},{12,16},{16,20},{20,24},{24,28},{28,0},{1,5},{5... | collective-permute-start | bytes 2654216 | tf_op jit(solution)/shard_map/ppermute | solution.py:40
  194.9 36.8 %copy-start.23 = (bf16[48,32,512]{2,1,0:T(8,128)(2,1)}, bf16[48,32,512]{2,1,0:T(8,128)(2,1)S(1)}, u32[]{:S(2)}) copy-start(bf16[48,32,512]{2,1,0:T(8,128)(2,1)S(1)} %get-tuple-element.47) | copy-start | bytes 4718596
  414.2 10.7 %collective-permute-start.9 = (f32[2,3,320]{1,2,0:T(8,128)S(1)}, f32[2,3,320]{1,2,0:T(8,128)S(1)}, u32[]{:S(2)}, u32[]{:S(2)}) collective-permute-start(f32[2,3,320]{1,2,0:T(8,128)S(1)} %pad_add_fusion.1), channel_id=1, source_target_pairs={{0,1},{1,2},{2,3},{4,5},{5,6},{6,7},{8,9},{9,10},{10,11},{12,13},{... | collective-permute-start | bytes 23048 | tf_op jit(solution)/shard_map/ppermute | solution.py:68
  419.0 14.9 %collective-permute-start.11 = (f32[2,3,512]{2,1,0:T(4,128)S(1)}, f32[2,3,512]{2,1,0:T(4,128)S(1)}, u32[]{:S(2)}, u32[]{:S(2)}) collective-permute-start(f32[2,3,512]{2,1,0:T(4,128)S(1)} %get-tuple-element.51), channel_id=1, source_target_pairs={{1,0},{2,1},{3,2},{5,4},{6,5},{7,6},{9,8},{10,9},{11,10},{13,12},{... | collective-permute-start | bytes 36872 | tf_op jit(solution)/shard_map/ppermute | solution.py:60
  420.2 13.7 %collective-permute-start.12 = (f32[2,3,512]{2,1,0:T(4,128)S(1)}, f32[2,3,512]{2,1,0:T(4,128)S(1)}, u32[]{:S(2)}, u32[]{:S(2)}) collective-permute-start(f32[2,3,512]{2,1,0:T(4,128)S(1)} %get-tuple-element.52), channel_id=1, source_target_pairs={{0,1},{1,2},{2,3},{4,5},{5,6},{6,7},{8,9},{9,10},{10,11},{12,13},{... | collective-permute-start | bytes 36872 | tf_op jit(solution)/shard_map/ppermute | solution.py:57
  454.6 121.2 %copy-start.71 = (pred[27]{0:T(512)(128)(4,1)S(1)}, pred[27]{0:T(512)(128)(4,1)}, u32[]{:S(2)}) copy-start(pred[27]{0:T(512)(128)(4,1)} %get-tuple-element.18) | copy-start | bytes 85
  (70 other events, 525.5 us)
Sparse Core Ops, SparseCore 0:
  373.6 188.5 all-reduce.9
